TPU v7x, 768 devices: a whole 4x8x12 slice. The times are simulated.
768 devices in a mesh: sec: 192 (over z_lo, x, y, core), col: 4 (over z_hi).
Axes of the slice: x: 4, y: 8, z: 12 (z_hi: 4, z_lo: 3; z = z_hi * 3 + z_lo), core: 2. Of those that a mesh axis runs over, the one named last changes fastest.
Arguments:
- air_state: float32 [4, 64, 786432], P(None, None, ('sec', 'col')), may hold values from -6 to 6
- air_mix: float32 [64, 786432], P(None, ('sec', 'col')), may hold values from 0.1 to 4
- surface_forcing: float32 [4, 786432], P(None, ('sec', 'col')), may hold values from 0 to 2
- air_mask: int32 [786432], P(('sec', 'col')), may hold values 0 or 1
- ocean_sources: int32 [4, 786432], P(None, ('sec', 'col')), may hold values from 0 to 6143, as said below
- ocean_weights: float32 [4, 786432], P(None, ('sec', 'col')), may hold values from 0.1 to 0.5
- sea_state: float32 [2, 80, 393216], P(None, None, ('sec', 'col')), may hold values from -6 to 6
- sea_mix: float32 [80, 393216], P(None, ('sec', 'col')), may hold values from 0.1 to 4
- ice_cover: float32 [393216], P(('sec', 'col')), may hold values from 0.05 to 0.95
- sea_mask: int32 [393216], P(('sec', 'col')), may hold values 0 or 1
- air_sources: int32 [4, 393216], P(None, ('sec', 'col')), may hold values from 0 to 12287, as said below
- air_weights: float32 [4, 393216], P(None, ('sec', 'col')), may hold values from 0.1 to 0.5
Outputs:
- air_out: float32 [4, 64, 786432], P(None, None, ('sec', 'col'))
- sea_out: float32 [2, 80, 393216], P(None, None, ('sec', 'col'))
- ice_out: float32 [393216], P(('sec', 'col'))
Inputs may be any that keep to these rules, and one draw needn't show every extreme that they name: Section t holds ocean cells t * 2048 to (t + 1) * 2048 - 1 and atmosphere columns t * 4096 to (t + 1) * 4096 - 1. An entry s of ocean_sources names cell s mod 2048 of the section s // 2048 - 1 places after the column's own. An entry s of air_sources names column s mod 4096 of the section s // 4096 - 1 places after the cell's own.
All inputs are finite; a program needn't handle non-finite values. No bound on the sum of `air_mask` or of `sea_mask` on one device may be relied on, other than what follows from the above.
Results may differ from a plain program's by a relative error of at most 0.0001.
Values sent between devices are 32-bit elements; how exact they have to be, the bound alone decides.
A program may use at most 64 MiB of HBM per device.

v0:
```python
import jax
import jax.numpy as jnp
from jax import lax
from jax.sharding import PartitionSpec as P

STEPS = 2


def extended(value, sides, width):
    for axis, dim in sides:
        peers, length = (lax.axis_size(axis), value.shape[dim])
        up = [(i, (i + 1) % peers) for i in range(peers)]
        down = [(j, i) for i, j in up]
        last = lax.slice_in_dim(value, length - width, length, axis=dim)
        leading = lax.slice_in_dim(value, 0, width, axis=dim)
        before = lax.ppermute(last, axis, up)
        after = lax.ppermute(leading, axis, down)
        value = jnp.concatenate([before, value, after], axis=dim)
    return value


def solve_columns(mixing, right_side):
    column_depth = mixing.shape[0]
    zeros_row = jnp.zeros_like(mixing[0])
    carry_c = zeros_row
    carry_d = jnp.zeros_like(right_side[:, 0])
    ratios = []
    reduced = []
    for depth_index in range(column_depth):
        lower_k = mixing[depth_index - 1] if depth_index > 0 else zeros_row
        upper_k = mixing[depth_index]
        pivot_value = 1.0 + lower_k + upper_k + lower_k * carry_c
        carry_c = -upper_k / pivot_value
        carry_d = (right_side[:, depth_index] + lower_k * carry_d) / pivot_value
        ratios.append(carry_c)
        reduced.append(carry_d)
    current = reduced[-1]
    solved = [current]
    for depth_index in range(column_depth - 2, -1, -1):
        current = reduced[depth_index] - ratios[depth_index] * current
        solved.append(current)
    return jnp.stack(solved[::-1], axis=1)


def remap(values, places, weights):
    return jnp.sum(weights[None] * values[:, places], axis=1)


def surface_fluxes(air_state, air_sea, surface_forcing, air_mask):
    bottom = air_state[:, 0]
    over_sea = air_mask == 1
    skin = jnp.where(over_sea, air_sea[0], surface_forcing[3])
    frozen = jnp.where(over_sea, air_sea[1], 0.0)
    speed = jnp.sqrt(bottom[2] * bottom[2] + bottom[3] * bottom[3] + 1.0)
    coefficient = 0.3 * speed / (1.0 + frozen)
    snow_part = 1.0 / (1.0 + jnp.exp(2.0 * skin))
    return jnp.stack(
        [
            coefficient * (skin - bottom[0]),
            coefficient * (0.5 * jnp.exp(0.3 * skin) - bottom[1]),
            coefficient * bottom[2],
            coefficient * bottom[3],
            surface_forcing[0] / (1.0 + frozen),
            surface_forcing[1] - 0.2 * skin,
            surface_forcing[2] * (1.0 - snow_part),
            surface_forcing[2] * snow_part,
        ]
    )


def air_step(air_state, air_mix, fluxes):
    bottom_add = jnp.stack([fluxes[0], fluxes[1], -fluxes[2], -fluxes[3]])
    return solve_columns(air_mix, air_state.at[:, 0].add(bottom_add))


def sea_step(sea_state, sea_mix, ice_cover, sea_mask, sea_flux):
    stress = jnp.sqrt(sea_flux[2] * sea_flux[2] + sea_flux[3] * sea_flux[3] + 0.01)
    heat = sea_flux[4] + sea_flux[5] - sea_flux[0] - sea_flux[1]
    open_water = 1.0 - ice_cover
    depth_decay = jnp.exp(-jnp.arange(sea_mix.shape[0], dtype=jnp.float32) / 8.0)
    mixing = sea_mix * (1.0 + 2.0 * stress[None, :] * depth_decay[:, None])
    top_add = jnp.stack(
        [0.5 * open_water * heat, 0.3 * open_water * (0.4 * sea_flux[1] - sea_flux[6])]
    )
    solved = solve_columns(mixing, sea_state.at[:, 0].add(top_add))
    wet_cells = sea_mask == 1
    new_state = jnp.where(wet_cells[None, None], solved, sea_state)
    grown = ice_cover / (ice_cover + open_water * jnp.exp(0.5 * heat - 0.8 * sea_flux[7]))
    return (new_state, jnp.where(wet_cells, grown, ice_cover))


def per_device(
    air_state,
    air_mix,
    surface_forcing,
    air_mask,
    ocean_sources,
    ocean_weights,
    sea_state,
    sea_mix,
    ice_cover,
    sea_mask,
    air_sources,
    air_weights,
):
    group_count = lax.axis_size("col")
    air_cols = air_state.shape[2]
    sea_cols = sea_state.shape[2]
    air_span = air_cols * group_count
    for step_index in range(STEPS):
        sea_top = jnp.stack([sea_state[0, 0], ice_cover])
        sea_block = lax.all_gather(sea_top, "col", axis=1, tiled=True)
        sea_nearby = extended(sea_block, (("sec", 1),), sea_cols * group_count)
        air_sea = remap(sea_nearby, ocean_sources, ocean_weights)
        fluxes = surface_fluxes(air_state, air_sea, surface_forcing, air_mask)
        flux_block = lax.all_gather(fluxes, "col", axis=1, tiled=True)
        flux_nearby = extended(flux_block, (("sec", 1),), air_span)
        air_state = air_step(air_state, air_mix, fluxes)
        sea_flux = remap(flux_nearby, air_sources, air_weights)
        sea_state, ice_cover = sea_step(sea_state, sea_mix, ice_cover, sea_mask, sea_flux)
    return (air_state, sea_state, ice_cover)


def solution(mesh):
    placed = (
        P(None, None, ("sec", "col")),
        P(None, ("sec", "col")),
        P(None, ("sec", "col")),
        P(("sec", "col")),
        P(None, ("sec", "col")),
        P(None, ("sec", "col")),
        P(None, None, ("sec", "col")),
        P(None, ("sec", "col")),
        P(("sec", "col")),
        P(("sec", "col")),
        P(None, ("sec", "col")),
        P(None, ("sec", "col")),
    )
    return jax.shard_map(
        per_device,
        mesh=mesh,
        in_specs=placed,
        out_specs=(P(None, None, ("sec", "col")), P(None, None, ("sec", "col")), P(("sec", "col"))),
        check_vma=False,
    )
```

profile of v0, /device:TPU:1, one launch (start us, length us, event | category | flops | bytes accessed | tf_op | source)
XLA Modules:
  0.0 295.4 jit_solution(15066903303966656255)
XLA Ops:
  2.1 22.2 %all_gather.12 = f32[2,2048]{1,0:T(2,128)S(1)} all-gather(f32[2,512]{1,0:T(2,128)S(1)} %pad_maximum_fusion.4), channel_id=1, replica_groups=mesh['sec'=192,'col'=4] {'col'}, dimensions={1}, use_global_device_ids=true | all-gather | bytes 20480 | tf_op jit(solution)/shard_map/all_gather | solution.py:112
  24.3 5.7 %collective-permute-start.1 = (f32[2,2048]{1,0:T(2,128)S(1)}, f32[2,2048]{1,0:T(2,128)S(1)}, u32[]{:S(2)}, u32[]{:S(2)}) collective-permute-start(f32[2,2048]{1,0:T(2,128)S(1)} %all_gather.12), channel_id=1, source_target_pairs={{4,0},{8,4},{12,8},{16,12},{20,16},{24,20},{28,24},{32,28},{36,32}... | collective-permute-start | bytes 49160 | tf_op jit(solution)/shard_map/ppermute | solution.py:17
  30.0 2.9 collective-permute-start
  38.7 2.9 negate_divide_fusion.20
  41.6 3.2 %fusion.452 = (f32[4,1,1024]{2,1,0:T(1,128)S(1)}, f32[4,1,1024]{2,1,0:T(1,128)}, f32[4,1,1024]{2,1,0:T(1,128)}, f32[4,1,1024]{2,1,0:T(1,128)}, f32[4,1,1024]{2,1...) fusion(f32[4,64,1024]{2,1,0:T(8,128)} %param.20), kind=kLoop, calls=%fused_computation.1762 | loop fusion | bytes 622592 | tf_op jit(solution)/shard_map/slice | solution.py:34
  44.8 3.4 %fusion.453 = (f32[4,1,1024]{2,1,0:T(1,128)}, f32[4,1,1024]{2,1,0:T(1,128)}, f32[4,1,1024]{2,1,0:T(1,128)}, f32[4,1,1024]{2,1,0:T(1,128)}, f32[4,1,1024]{2,1,0:T...) fusion(f32[4,64,1024]{2,1,0:T(8,128)} %param.20), kind=kLoop, calls=%fused_computation.1763 | loop fusion | bytes 622592 | tf_op jit(solution)/shard_map/slice | solution.py:34
  54.1 3.3 %fusion.451 = (f32[4,1,1024]{2,1,0:T(1,128)}, f32[4,1,1024]{2,1,0:T(1,128)S(1)}, f32[4,1,1024]{2,1,0:T(1,128)}, f32[4,1,1024]{2,1,0:T(1,128)}, f32[4,1,1024]{2,1...) fusion(f32[4,64,1024]{2,1,0:T(8,128)} %param.20), kind=kLoop, calls=%fused_computation.1761 | loop fusion | bytes 622592 | tf_op jit(solution)/shard_map/slice | solution.py:34
  89.5 15.4 %gather_fusion = f32[4096,2]{1,0:T(8,128)} fusion(f32[2,6144]{0,1:T(8,128)S(1)} %copy.754, s32[4096]{0:T(1024)} %bitcast_clamp_fusion), kind=kCustom, calls=%fused_computation | custom fusion | bytes 81920 | tf_op jit(solution)/shard_map/gather | solution.py:46
  110.1 13.0 %all_gather.13 = f32[8,4096]{1,0:T(8,128)S(1)} all-gather(f32[8,1024]{1,0:T(8,128)S(1)} %stack.715), channel_id=1, replica_groups=mesh['sec'=192,'col'=4] {'col'}, dimensions={1}, use_global_device_ids=true | all-gather | bytes 163840 | tf_op jit(solution)/shard_map/all_gather | solution.py:116
  123.1 8.6 %collective-permute-start.3 = (f32[8,4096]{1,0:T(8,128)S(1)}, f32[8,4096]{1,0:T(8,128)S(1)}, u32[]{:S(2)}, u32[]{:S(2)}) collective-permute-start(f32[8,4096]{1,0:T(8,128)S(1)} %all_gather.13), channel_id=1, source_target_pairs={{4,0},{8,4},{12,8},{16,12},{20,16},{24,20},{28,24},{32,28},{36,32}... | collective-permute-start | bytes 393224 | tf_op jit(solution)/shard_map/ppermute | solution.py:17
  136.4 3.7 %multiply_subtract_fusion.103 = (f32[4,1024]{1,0:T(4,128)S(1)}, f32[4,1024]{1,0:T(4,128)}, f32[4,1024]{1,0:T(4,128)}, f32[4,1024]{1,0:T(4,128)}, f32[4,1024]{1,0...) fusion(f32[4,1024]{1,0:T(4,128)S(1)} %get-tuple-element.742, ...), kind=kLoop, calls=%fused_computation.712 | loop fusion | flops 1200128 | bytes 2097152 | tf_op jit(solution)/shard_map/sub | solution.py:40
  142.8 3.9 %copy.819 = f32[8,12288]{0,1:T(8,128)} copy(f32[8,12288]{1,0:T(8,128)S(1)} %pad_maximum_fusion) | data formatting | bytes 786432 | tf_op jit(solution)/shard_map/concatenate | solution.py:18
  146.8 8.3 %gather_fusion.1 = f32[2048,8]{1,0:T(8,128)S(1)} fusion(f32[8,12288]{0,1:T(8,128)} %copy.819, s32[2048]{0:T(1024)S(1)} %copy-done.205), kind=kCustom, calls=%fused_computation.1 | custom fusion | bytes 139264 | tf_op jit(solution)/shard_map/gather | solution.py:46
  160.9 12.7 %all_gather.14 = f32[2,2048]{1,0:T(2,128)S(1)} all-gather(f32[2,512]{1,0:T(2,128)S(1)} %pad_maximum_fusion.5), channel_id=1, replica_groups=mesh['sec'=192,'col'=4] {'col'}, dimensions={1}, use_global_device_ids=true | all-gather | bytes 20480 | tf_op jit(solution)/shard_map/all_gather | solution.py:112
  173.6 10.9 %collective-permute-start.5 = (f32[2,2048]{1,0:T(2,128)S(1)}, f32[2,2048]{1,0:T(2,128)S(1)}, u32[]{:S(2)}, u32[]{:S(2)}) collective-permute-start(f32[2,2048]{1,0:T(2,128)S(1)} %all_gather.14), channel_id=1, source_target_pairs={{4,0},{8,4},{12,8},{16,12},{20,16},{24,20},{28,24},{32,28},{36,32}... | collective-permute-start | bytes 49160 | tf_op jit(solution)/shard_map/ppermute | solution.py:17
  187.0 3.2 %collective-permute-done.4 = f32[2,2048]{1,0:T(2,128)S(1)} collective-permute-done((f32[2,2048]{1,0:T(2,128)S(1)}, f32[2,2048]{1,0:T(2,128)S(1)}, u32[]{:S(2)}, u32[]{:S(2)}) %collective-permute-start.4) | collective-permute-done | bytes 16416 | tf_op jit(solution)/shard_map/ppermute | solution.py:16
  192.6 15.4 %gather_fusion.2 = f32[4096,2]{1,0:T(8,128)} fusion(f32[2,6144]{0,1:T(8,128)S(1)} %copy.901, s32[4096]{0:T(1024)} %bitcast_clamp_fusion), kind=kCustom, calls=%fused_computation.2 | custom fusion | bytes 81920 | tf_op jit(solution)/shard_map/gather | solution.py:46
  213.1 13.5 %all_gather.15 = f32[8,4096]{1,0:T(8,128)S(1)} all-gather(f32[8,1024]{1,0:T(8,128)S(1)} %stack.831), channel_id=1, replica_groups=mesh['sec'=192,'col'=4] {'col'}, dimensions={1}, use_global_device_ids=true | all-gather | bytes 163840 | tf_op jit(solution)/shard_map/all_gather | solution.py:116
  226.5 13.5 %collective-permute-start.7 = (f32[8,4096]{1,0:T(8,128)S(1)}, f32[8,4096]{1,0:T(8,128)S(1)}, u32[]{:S(2)}, u32[]{:S(2)}) collective-permute-start(f32[8,4096]{1,0:T(8,128)S(1)} %all_gather.15), channel_id=1, source_target_pairs={{4,0},{8,4},{12,8},{16,12},{20,16},{24,20},{28,24},{32,28},{36,32}... | collective-permute-start | bytes 393224 | tf_op jit(solution)/shard_map/ppermute | solution.py:17
  242.6 3.1 %add_divide_fusion.38 = (f32[4,1,1024]{2,0,1:T(4,128)S(1)}, f32[4,1,1024]{2,0,1:T(4,128)S(1)}, f32[4,1,1024]{2,0,1:T(4,128)S(1)}, f32[4,1,1024]{2,0,1:T(4,128)S(...) fusion(f32[1024]{0:T(1024)} %bitcast.3545, ...), kind=kLoop, calls=%fused_computation.586 | loop fusion | flops 1093632 | bytes 2232320 | tf_op jit(solution)/shard_map/div | solution.py:34
  248.1 2.6 constant_dynamic-update-slice_fusion.143
  251.1 3.4 %constant_dynamic-update-slice_fusion.142 = (f32[4,64,1024]{2,0,1:T(4,128)S(1)}, f32[4,1,1024]{2,0,1:T(4,128)S(1)}, f32[4,1,1024]{2,0,1:T(4,128)S(1)}, f32[4,1,1...) fusion(f32[4,64,1024]{2,0,1:T(4,128)S(1)} %get-tuple-element.40, ...), kind=kLoop, calls=%fused_computation.154 | loop fusion | flops 1454080 | bytes 2519040
  276.1 4.2 %copy.902 = f32[8,12288]{0,1:T(8,128)} copy(f32[8,12288]{1,0:T(8,128)S(1)} %pad_maximum_fusion.1) | data formatting | bytes 786432 | tf_op jit(solution)/shard_map/concatenate | solution.py:18
  280.3 8.3 %gather_fusion.3 = f32[2048,8]{1,0:T(8,128)S(1)} fusion(f32[8,12288]{0,1:T(8,128)} %copy.902, s32[2048]{0:T(1024)S(1)} %copy-done.206), kind=kCustom, calls=%fused_computation.3 | custom fusion | bytes 139264 | tf_op jit(solution)/shard_map/gather | solution.py:46
  (838 shorter events, 102.7 us)
Async XLA Ops:
  0.6 56.7 %copy-start.211 = (f32[4,1024]{1,0:T(4,128)S(1)}, f32[4,1024]{1,0:T(4,128)}, u32[]{:S(2)}) copy-start(f32[4,1024]{1,0:T(4,128)} %param.22) | copy-start | bytes 49156
  0.6 57.3 %copy-start.212 = (s32[4,1024]{1,0:T(4,128)S(1)}, s32[4,1024]{1,0:T(4,128)}, u32[]{:S(2)}) copy-start(s32[4,1024]{1,0:T(4,128)} %param.24) | copy-start | bytes 49156
  0.7 57.9 %copy-start.216 = (s32[4,512]{1,0:T(4,128)S(1)}, s32[4,512]{1,0:T(4,128)}, u32[]{:S(2)}) copy-start(s32[4,512]{1,0:T(4,128)} %param.30) | copy-start | bytes 24580
  24.3 62.6 %collective-permute-start.1 = (f32[2,2048]{1,0:T(2,128)S(1)}, f32[2,2048]{1,0:T(2,128)S(1)}, u32[]{:S(2)}, u32[]{:S(2)}) collective-permute-start(f32[2,2048]{1,0:T(2,128)S(1)} %all_gather.12), channel_id=1, source_target_pairs={{4,0},{8,4},{12,8},{16,12},{20,16},{24,20},{28,24},{32,28},{36,32}... | collective-permute-start | bytes 49160 | tf_op jit(solution)/shard_map/ppermute | solution.py:17
  30.0 56.9 %collective-permute-start = (f32[2,2048]{1,0:T(2,128)S(1)}, f32[2,2048]{1,0:T(2,128)S(1)}, u32[]{:S(2)}, u32[]{:S(2)}) collective-permute-start(f32[2,2048]{1,0:T(2,128)S(1)} %all_gather.12), channel_id=1, source_target_pairs={{0,4},{4,8},{8,12},{12,16},{16,20},{20,24},{24,28},{28,32},{32,36}... | collective-permute-start | bytes 49160 | tf_op jit(solution)/shard_map/ppermute | solution.py:16
  34.8 51.9 %copy-start.50 = (f32[1,1024]{1,0:T(1,128)}, f32[1,1024]{1,0:T(1,128)S(1)}, u32[]{:S(2)}) copy-start(f32[1,1024]{1,0:T(1,128)S(1)} %get-tuple-element.988) | copy-start | bytes 12292
  34.8 51.9 %copy-start.53 = (f32[1,1024]{1,0:T(1,128)}, f32[1,1024]{1,0:T(1,128)S(1)}, u32[]{:S(2)}) copy-start(f32[1,1024]{1,0:T(1,128)S(1)} %get-tuple-element.990) | copy-start | bytes 12292
  34.8 51.9 %copy-start.56 = (f32[1,1024]{1,0:T(1,128)}, f32[1,1024]{1,0:T(1,128)S(1)}, u32[]{:S(2)}) copy-start(f32[1,1024]{1,0:T(1,128)S(1)} %get-tuple-element.992) | copy-start | bytes 12292
  34.8 51.9 %copy-start.59 = (f32[1,1024]{1,0:T(1,128)}, f32[1,1024]{1,0:T(1,128)S(1)}, u32[]{:S(2)}) copy-start(f32[1,1024]{1,0:T(1,128)S(1)} %get-tuple-element.994) | copy-start | bytes 12292
  34.8 51.9 %copy-start.62 = (f32[1,1024]{1,0:T(1,128)}, f32[1,1024]{1,0:T(1,128)S(1)}, u32[]{:S(2)}) copy-start(f32[1,1024]{1,0:T(1,128)S(1)} %get-tuple-element.996) | copy-start | bytes 12292
  34.8 51.9 %copy-start.65 = (f32[1,1024]{1,0:T(1,128)}, f32[1,1024]{1,0:T(1,128)S(1)}, u32[]{:S(2)}) copy-start(f32[1,1024]{1,0:T(1,128)S(1)} %get-tuple-element.998) | copy-start | bytes 12292
  34.8 51.9 %copy-start.123 = (f32[1,1024]{1,0:T(1,128)}, f32[1,1024]{1,0:T(1,128)S(1)}, u32[]{:S(2)}) copy-start(f32[1,1024]{1,0:T(1,128)S(1)} %get-tuple-element.982) | copy-start | bytes 12292
  34.8 51.9 %copy-start.188 = (f32[1,1024]{1,0:T(1,128)}, f32[1,1024]{1,0:T(1,128)S(1)}, u32[]{:S(2)}) copy-start(f32[1,1024]{1,0:T(1,128)S(1)} %get-tuple-element.989) | copy-start | bytes 12292
  34.8 51.9 %copy-start.190 = (f32[1,1024]{1,0:T(1,128)}, f32[1,1024]{1,0:T(1,128)S(1)}, u32[]{:S(2)}) copy-start(f32[1,1024]{1,0:T(1,128)S(1)} %get-tuple-element.993) | copy-start | bytes 12292
  34.9 51.9 %copy-start.192 = (f32[1,1024]{1,0:T(1,128)}, f32[1,1024]{1,0:T(1,128)S(1)}, u32[]{:S(2)}) copy-start(f32[1,1024]{1,0:T(1,128)S(1)} %get-tuple-element.997) | copy-start | bytes 12292
  34.9 51.6 %copy-start = (f32[2,80,512]{2,1,0:T(8,128)S(1)}, f32[2,80,512]{2,1,0:T(8,128)}, u32[]{:S(2)}) copy-start(f32[2,80,512]{2,1,0:T(8,128)} %param.26) | copy-start | bytes 983044
  36.8 50.0 %copy-start.68 = (f32[1,1024]{1,0:T(1,128)}, f32[1,1024]{1,0:T(1,128)S(1)}, u32[]{:S(2)}) copy-start(f32[1,1024]{1,0:T(1,128)S(1)} %get-tuple-element.1001) | copy-start | bytes 12292
  36.8 50.0 %copy-start.71 = (f32[1,1024]{1,0:T(1,128)}, f32[1,1024]{1,0:T(1,128)S(1)}, u32[]{:S(2)}) copy-start(f32[1,1024]{1,0:T(1,128)S(1)} %get-tuple-element.1003) | copy-start | bytes 12292
  123.1 19.7 %collective-permute-start.3 = (f32[8,4096]{1,0:T(8,128)S(1)}, f32[8,4096]{1,0:T(8,128)S(1)}, u32[]{:S(2)}, u32[]{:S(2)}) collective-permute-start(f32[8,4096]{1,0:T(8,128)S(1)} %all_gather.13), channel_id=1, source_target_pairs={{4,0},{8,4},{12,8},{16,12},{20,16},{24,20},{28,24},{32,28},{36,32}... | collective-permute-start | bytes 393224 | tf_op jit(solution)/shard_map/ppermute | solution.py:17
  131.6 11.1 %collective-permute-start.2 = (f32[8,4096]{1,0:T(8,128)S(1)}, f32[8,4096]{1,0:T(8,128)S(1)}, u32[]{:S(2)}, u32[]{:S(2)}) collective-permute-start(f32[8,4096]{1,0:T(8,128)S(1)} %all_gather.13), channel_id=1, source_target_pairs={{0,4},{4,8},{8,12},{12,16},{16,20},{20,24},{24,28},{28,32},{32,36}... | collective-permute-start | bytes 393224 | tf_op jit(solution)/shard_map/ppermute | solution.py:16
  173.6 13.4 %collective-permute-start.5 = (f32[2,2048]{1,0:T(2,128)S(1)}, f32[2,2048]{1,0:T(2,128)S(1)}, u32[]{:S(2)}, u32[]{:S(2)}) collective-permute-start(f32[2,2048]{1,0:T(2,128)S(1)} %all_gather.14), channel_id=1, source_target_pairs={{4,0},{8,4},{12,8},{16,12},{20,16},{24,20},{28,24},{32,28},{36,32}... | collective-permute-start | bytes 49160 | tf_op jit(solution)/shard_map/ppermute | solution.py:17
  184.4 5.7 %collective-permute-start.4 = (f32[2,2048]{1,0:T(2,128)S(1)}, f32[2,2048]{1,0:T(2,128)S(1)}, u32[]{:S(2)}, u32[]{:S(2)}) collective-permute-start(f32[2,2048]{1,0:T(2,128)S(1)} %all_gather.14), channel_id=1, source_target_pairs={{0,4},{4,8},{8,12},{12,16},{16,20},{20,24},{24,28},{28,32},{32,36}... | collective-permute-start | bytes 49160 | tf_op jit(solution)/shard_map/ppermute | solution.py:16
  226.5 49.5 %collective-permute-start.7 = (f32[8,4096]{1,0:T(8,128)S(1)}, f32[8,4096]{1,0:T(8,128)S(1)}, u32[]{:S(2)}, u32[]{:S(2)}) collective-permute-start(f32[8,4096]{1,0:T(8,128)S(1)} %all_gather.15), channel_id=1, source_target_pairs={{4,0},{8,4},{12,8},{16,12},{20,16},{24,20},{28,24},{32,28},{36,32}... | collective-permute-start | bytes 393224 | tf_op jit(solution)/shard_map/ppermute | solution.py:17
  240.1 35.9 %collective-permute-start.6 = (f32[8,4096]{1,0:T(8,128)S(1)}, f32[8,4096]{1,0:T(8,128)S(1)}, u32[]{:S(2)}, u32[]{:S(2)}) collective-permute-start(f32[8,4096]{1,0:T(8,128)S(1)} %all_gather.15), channel_id=1, source_target_pairs={{0,4},{4,8},{8,12},{12,16},{16,20},{20,24},{24,28},{28,32},{32,36}... | collective-permute-start | bytes 393224 | tf_op jit(solution)/shard_map/ppermute | solution.py:16
  (205 other events, 4223.3 us)
where the time goes:
time: 300 us; the launch traced here: 295 us
  other arithmetic  91.4 us (30%)
  local copies, waits for them, and re-layouts  86.3 us (29%)
  blocking collectives  61.3 us (20%)
  starting transfers between devices  47.7 us (16%)
  between operations  5.51 us (2%)
  waiting for transfers between devices  3.17 us (1%)
    gather x4, local copies, waits for them, and re-layouts, remap(): return jnp.sum(weights[None] * values[:, places], axis=1)  47.4 us
    ppermute x4, starting transfers between devices, extended(): after = lax.ppermute(leading, axis, down)  38.7 us
    all_gather x2, blocking collectives, per_device(): sea_block = lax.all_gather(sea_top, 'col', axis=1, tiled=True)  34.9 us
    unnamed x114, other arithmetic  28.9 us
    all_gather x2, blocking collectives, per_device(): flux_block = lax.all_gather(fluxes, 'col', axis=1, tiled=True)  26.4 us
    add x22, other arithmetic, solve_columns(): pivot_value = 1.0 + lower_k + upper_k + lower_k * carry_c  26.1 us
    slice x4, local copies, waits for them, and re-layouts, solve_columns(): carry_d = (right_side[:, depth_index] + lower_k * carry_d) / pivot_value  12.2 us
    concatenate x4, local copies, waits for them, and re-layouts, extended(): value = jnp.concatenate([before, value, after], axis=dim)  11.7 us
  transfers between devices with their start and end apart: 8, of which 1 were waited for; matrix products, arithmetic and copies ran while one was open for 32% of the time, Pallas kernels for 0%

commit v1 on v0

v1 whole, which is shorter than its diff:
```python
import functools

import jax
import jax.numpy as jnp
from jax import lax
from jax.experimental import pallas as pl
from jax.experimental.pallas import tpu as pltpu
from jax.sharding import PartitionSpec as P

STEPS = 2
COLS = 4
LEV = 64
OLEV = 80
MESH = pl.DeviceIdType.MESH
F32 = jnp.float32
GATHER = lax.GatherDimensionNumbers(
    offset_dims=(),
    collapsed_slice_dims=(1,),
    start_index_map=(1,),
    operand_batching_dims=(0,),
    start_indices_batching_dims=(0,),
)


def lanes(row, index):
    return lax.gather(
        jnp.broadcast_to(row, (8, 128)),
        index[:, :, None],
        GATHER,
        slice_sizes=(1, 1),
        mode=lax.GatherScatterMode.PROMISE_IN_BOUNDS,
    )


def twice(half):
    return jnp.concatenate([half, half], axis=0)


def kernel(
    sections,
    air_h, amix_h, forcing_h, amask_h, osrc_h, owt_h, sea_h, smix_h, ice_h, smask_h, asrc_h, awt_h,
    air_o, sea_o, ice_o,
    air_v, amix_v, forcing_v, amask_v, osrc_v, owt_v, sea_v, smix_v, ice_v, smask_v, asrc_v, awt_v,
    top_out, top_in, flux_in, part_acc, part_out, part_in,
    smix8, sdecay8, sea8, sq, sw, sa, sb,
    aq, aa, ag, ab, ae, ay, aw, air_w, sea_w, ice_w,
    load_sem, src_send, src_recv, wt_send, wt_recv,
    top_send, top_recv, flux_send, flux_recv, part_send, part_recv, out_sem,
):
    sec = lax.axis_index("sec")
    col = lax.axis_index("col")

    def peer(shift, turn):
        return (lax.rem(sec + shift + sections, sections), lax.rem(col + turn, COLS))

    others = [(s, t) for t in (2, 1, 3, 0) for s in (0, -1, 1) if (s, t) != (0, 0)]

    barrier = pltpu.get_barrier_semaphore()
    for place in others:
        pl.semaphore_signal(barrier, inc=1, device_id=peer(*place), device_id_type=MESH)

    loads = [
        pltpu.make_async_copy(src, dst, load_sem.at[i])
        for i, (src, dst) in enumerate(
            [
                (sea_h, sea_v), (ice_h, ice_v), (osrc_h, osrc_v), (owt_h, owt_v),
                (forcing_h, forcing_v), (amask_h, amask_v), (amix_h, amix_v), (air_h, air_v),
                (smix_h, smix_v), (smask_h, smask_v),
                (asrc_h, asrc_v.at[col]), (awt_h, awt_v.at[col]),
            ]
        )
    ]
    for load in loads:
        load.start()

    first = lax.broadcasted_iota(jnp.int32, (8, 128), 0) < 4
    waiting = []

    def send_top(step):
        for n, (shift, turn) in enumerate(others):
            copy = pltpu.make_async_remote_copy(
                src_ref=top_out.at[step],
                dst_ref=top_in.at[step, (1 - shift) * COLS + col],
                send_sem=top_send.at[step, n],
                recv_sem=top_recv.at[step, (1 - shift) * COLS + col],
                device_id=peer(shift, turn),
                device_id_type=MESH,
            )
            copy.start()
            waiting.append(copy)

    loads[0].wait()
    loads[1].wait()
    top_out[0] = jnp.concatenate([sea_v[pl.ds(0, 4, stride=8), :], ice_v[...]], axis=0)
    pl.semaphore_wait(barrier, len(others))
    send_top(0)
    for turn in (2, 1, 3):
        for src, dst, send, recv in ((asrc_h, asrc_v, src_send, src_recv), (awt_h, awt_v, wt_send, wt_recv)):
            copy = pltpu.make_async_remote_copy(
                src_ref=src,
                dst_ref=dst.at[col],
                send_sem=send.at[turn],
                recv_sem=recv.at[col],
                device_id=peer(0, turn),
                device_id_type=MESH,
            )
            copy.start()
            waiting.append(copy)

    for load in loads[2:10]:
        load.wait()

    def air_up(n, carry):
        tile = 7 - n
        p, q = carry
        for s in range(7, -1, -1):
            k = amix_v[pl.ds(tile * 64 + s, 8, stride=8), :]
            b = 1.0 / (1.0 + k)
            a = k * b
            aq_next = q
            flow = a * q
            q = b * p + flow
            p = p + flow
            level = pl.ds(pl.multiple_of(tile * 64 + s * 8, 8), 8)
            below = pl.ds(pl.multiple_of(tile * 64 + s * 8 + 8, 8), 8)
            aq[level, :] = q
            aa[level, :] = a
            r = 1.0 / q
            ag[below, :] = a * aq_next * r
            ab[below, :] = b * r
        return p, q

    one = jnp.ones((8, 128), F32)
    zero = jnp.zeros((8, 128), F32)
    pa, qa = lax.fori_loop(0, LEV // 8, air_up, (one, zero))
    inv_pa = 1.0 / pa

    def air_solve(load):
        def up(n, w):
            tile = 7 - n
            w = list(w)
            for s in range(7, -1, -1):
                row = pl.multiple_of(tile * 64 + s * 8, 8)
                q, a = aq[pl.ds(row, 8), :], aa[pl.ds(row, 8), :]
                e = load(tile, s)
                for f in range(4):
                    w[f] = q * e[f] + a * w[f]
                    aw[f, pl.ds(row, 8), :] = w[f]
            return tuple(w)

        return [v * inv_pa for v in lax.fori_loop(0, LEV // 8, up, (zero,) * 4)]

    def from_start(tile, s):
        return [air_v[pl.ds(f * 512 + tile * 64 + s, 8, stride=8), :] for f in range(4)]

    top = air_solve(from_start)
    unit = qa * inv_pa

    def air_down(tile, carry):
        x, e = list(carry[:4]), carry[4]
        for s in range(8):
            row = pl.multiple_of(tile * 64 + s * 8, 8)
            g, b = ag[pl.ds(row, 8), :], ab[pl.ds(row, 8), :]
            for f in range(4):
                x[f] = g * x[f] + b * aw[f, pl.ds(row, 8), :]
                ay[f, pl.ds(row, 8), :] = x[f]
            e = g * e
            ae[pl.ds(row, 8), :] = e
        return (*x, e)

    ag[pl.ds(0, 8), :] = one
    ab[pl.ds(0, 8), :] = zero
    lax.fori_loop(0, LEV // 8, air_down, (*top, unit))

    def sea_prepare(tile, carry):
        decay = jnp.exp(jnp.full((8, 128), -tile.astype(F32)))
        for s in range(8):
            row = pl.ds(pl.multiple_of(tile * 64 + s * 8, 8), 8)
            k = twice(smix_v[pl.ds(tile * 32 + s, 4, stride=8), :])
            smix8[row, :] = k
            sdecay8[row, :] = k * (decay * jnp.exp(jnp.full((8, 128), -s / 8.0, F32)))
            sea8[row, :] = jnp.concatenate(
                [sea_v[pl.ds(tile * 32 + s, 4, stride=8), :], sea_v[pl.ds(320 + tile * 32 + s, 4, stride=8), :]], axis=0
            )
        return carry

    lax.fori_loop(0, OLEV // 8, sea_prepare, 0)
    wet = twice(smask_v[...]) == 1
    ice = twice(ice_v[...])
    over_sea = amask_v[...] == 1
    forcing = [forcing_v[pl.ds(f, 8, stride=4), :] for f in range(4)]
    bottom = [air_v[pl.ds(f * 512, 8, stride=8), :] for f in range(4)]

    push = None
    for step in range(STEPS):
        last = step == STEPS - 1
        top_in[step, COLS + col] = top_out[step]
        source = [osrc_v[pl.ds(k, 8, stride=4), :] for k in range(4)]
        lane = [v & 127 for v in source]
        line = [v >> 7 for v in source]
        temps, ices = [zero] * 4, [zero] * 4
        for shift, turn in [(0, 0), *[(s, t) for t in (0, 1, 3, 2) for s in (0, -1, 1) if (s, t) != (0, 0)]]:
            slot = (1 + shift) * COLS + lax.rem(col + turn, COLS)
            if (shift, turn) != (0, 0):
                pltpu.make_async_copy(top_in.at[step, slot], top_in.at[step, slot], top_recv.at[step, slot]).wait()
            for c in range(4):
                t, i = top_in[step, slot, pl.ds(c, 1), :], top_in[step, slot, pl.ds(4 + c, 1), :]
                for k in range(4):
                    here = line[k] == slot * 4 + c
                    temps[k] = jnp.where(here, lanes(t, lane[k]), temps[k])
                    ices[k] = jnp.where(here, lanes(i, lane[k]), ices[k])
        weight = [owt_v[pl.ds(k, 8, stride=4), :] for k in range(4)]
        warm = (weight[0] * temps[0] + weight[1] * temps[1]) + (weight[2] * temps[2] + weight[3] * temps[3])
        cold = (weight[0] * ices[0] + weight[1] * ices[1]) + (weight[2] * ices[2] + weight[3] * ices[3])

        skin = jnp.where(over_sea, warm, forcing[3])
        frozen = jnp.where(over_sea, cold, 0.0)
        closed = 1.0 / (1.0 + frozen)
        speed = jnp.sqrt(bottom[2] * bottom[2] + bottom[3] * bottom[3] + 1.0)
        coef = 0.3 * speed * closed
        snow = 1.0 / (1.0 + jnp.exp(2.0 * skin))
        f0 = coef * (skin - bottom[0])
        f1 = coef * (0.5 * jnp.exp(0.3 * skin) - bottom[1])
        f2 = coef * bottom[2]
        f3 = coef * bottom[3]
        heat = forcing[0] * closed + (forcing[1] - 0.2 * skin) - f0 - f1
        salt = 0.4 * f1 - forcing[2] * (1.0 - snow)
        melt = 0.5 * heat - 0.8 * (forcing[2] * snow)
        for f, v in enumerate((f2, f3, heat, salt, melt)):
            flux_in[step, 1, f] = v
        for n, shift in enumerate((-1, 1)):
            copy = pltpu.make_async_remote_copy(
                src_ref=flux_in.at[step, 1],
                dst_ref=flux_in.at[step, 1 - shift],
                send_sem=flux_send.at[step, n],
                recv_sem=flux_recv.at[step, 1 - shift],
                device_id=peer(shift, 0),
                device_id_type=MESH,
            )
            copy.start()
            waiting.append(copy)
        push = (f0, f1, -f2, -f3)

        if step == 0:
            loads[10].wait()
            loads[11].wait()
            for turn in (1, 2, 3):
                slot = lax.rem(col + turn, COLS)
                pltpu.make_async_copy(asrc_v.at[slot], asrc_v.at[slot], src_recv.at[slot]).wait()
                pltpu.make_async_copy(awt_v.at[slot], awt_v.at[slot], wt_recv.at[slot]).wait()

        def picked(target, bands, sums):
            index = [asrc_v[target, pl.ds(8 * h, 8), :] for h in range(2)]
            lane = [v & 127 for v in index]
            line = [(v >> 7) - 8 * col for v in index]
            for band in bands:
                for j in range(8):
                    here = [line[h] == band * 32 + j for h in range(2)]
                    for f in range(5):
                        row = flux_in[step, band, f, pl.ds(j, 1), :]
                        for h in range(2):
                            sums[f * 2 + h] = jnp.where(here[h], lanes(row, lane[h]), sums[f * 2 + h])
            return sums

        def own_part(turn, carry):
            target = lax.rem(col + turn, COLS)
            for n, v in enumerate(picked(target, (1,), [zero] * 10)):
                part_acc[turn, n] = v
            return carry

        lax.fori_loop(0, COLS, own_part, 0)
        if last:
            def air_result(tile, carry):
                for s in range(8):
                    row = pl.multiple_of(tile * 64 + s * 8, 8)
                    e = ae[pl.ds(row, 8), :]
                    for f in range(4):
                        air_w[pl.ds(f * 512 + tile * 64 + s, 8, stride=8), :] = ay[f, pl.ds(row, 8), :] + e * push[f]
                return carry

            lax.fori_loop(0, LEV // 8, air_result, 0)
            air_copy = pltpu.make_async_copy(air_w, air_o, out_sem.at[0])
            air_copy.start()

        for band in (0, 2):
            pltpu.make_async_copy(flux_in.at[step, band], flux_in.at[step, band], flux_recv.at[step, band]).wait()

        def whole_part(target, turn):
            sums = picked(target, (0, 2), [part_acc[turn, n] for n in range(10)])
            for f in range(5):
                done = []
                for h in range(2):
                    v = sums[f * 2 + h] * awt_v[target, pl.ds(8 * h, 8), :]
                    v = v + pltpu.roll(v, 6, 0)
                    v = v + pltpu.roll(v, 7, 0)
                    done.append(v)
                part_out[step, turn, pl.ds(4 * f, 4), :] = jnp.concatenate(
                    [done[0][0:1], done[0][4:5], done[1][0:1], done[1][4:5]], axis=0
                )

        for turn in (2, 1, 3, 0):
            target = lax.rem(col + turn, COLS)
            whole_part(target, turn)
            if turn:
                copy = pltpu.make_async_remote_copy(
                    src_ref=part_out.at[step, turn],
                    dst_ref=part_in.at[step, COLS - turn],
                    send_sem=part_send.at[step, turn],
                    recv_sem=part_recv.at[step, COLS - turn],
                    device_id=peer(0, turn),
                    device_id_type=MESH,
                )
                copy.start()
                waiting.append(copy)

        if not last:
            bottom = [ay[f, pl.ds(0, 8), :] + ae[pl.ds(0, 8), :] * push[f] for f in range(4)]
            first_push = push

            def after_first(tile, s):
                row = pl.multiple_of(tile * 64 + s * 8, 8)
                return [ay[f, pl.ds(row, 8), :] + ae[pl.ds(row, 8), :] * first_push[f] for f in range(4)]

            top = air_solve(after_first)

        total = part_out[step, 0]
        for turn in (1, 3, 2):
            pltpu.make_async_copy(part_in.at[step, turn], part_in.at[step, turn], part_recv.at[step, turn]).wait()
            total = total + part_in[step, turn]
        f2, f3, heat, salt, melt = [total[4 * f : 4 * f + 4] for f in range(5)]

        stress = twice(2.0 * jnp.sqrt(f2 * f2 + f3 * f3 + 0.01))
        open_water = 1.0 - ice
        added = open_water * jnp.concatenate([0.5 * heat, 0.3 * salt], axis=0)
        sea8[pl.ds(0, 8), :] = sea8[pl.ds(0, 8), :] + jnp.where(wet, added, 0.0)

        def sea_up(n, carry):
            tile = OLEV // 8 - 1 - n
            p, q, w = carry
            for s in range(7, -1, -1):
                row = pl.ds(pl.multiple_of(tile * 64 + s * 8, 8), 8)
                k = smix8[row, :] + stress * sdecay8[row, :]
                b = 1.0 / (1.0 + k)
                a = k * b
                flow = a * q
                q = b * p + flow
                p = p + flow
                w = q * sea8[row, :] + a * w
                sa[row, :] = a
                sb[row, :] = b
                sq[row, :] = q
                sw[row, :] = w
            return p, q, w

        p, q, w = lax.fori_loop(0, OLEV // 8, sea_up, (one, zero, zero))
        surface = jnp.where(wet, w / p, sea8[pl.ds(0, 8), :])
        grown = ice / (ice + open_water * jnp.exp(twice(melt)))
        ice = jnp.where(wet, grown, ice)
        if not last:
            top_out[step + 1] = jnp.where(first, surface, ice)
            send_top(step + 1)
            lax.fori_loop(0, LEV // 8, functools.partial(air_down_again, ag, ab, aw, ay), tuple(top))
        else:
            ice_w[...] = ice[0:4]
            ice_copy = pltpu.make_async_copy(ice_w, ice_o, out_sem.at[2])
            ice_copy.start()

        def sea_level(row, x, q, a, b):
            here = sq[row, :]
            r = 1.0 / q
            x = (a * here * r) * x + (b * r) * sw[row, :]
            return x, here, sa[row, :], sb[row, :]

        def sea_keep(row, tile, s, x):
            x = jnp.where(wet, x, sea8[row, :])
            if last:
                sea_w[pl.ds(tile * 32 + s, 4, stride=8), :] = x[0:4]
                sea_w[pl.ds(320 + tile * 32 + s, 4, stride=8), :] = x[4:8]
            else:
                sea8[row, :] = x

        def sea_down(tile, carry):
            x, q, a, b = carry
            for s in range(8):
                row = pl.ds(pl.multiple_of(tile * 64 + s * 8, 8), 8)
                x, q, a, b = sea_level(row, x, q, a, b)
                sea_keep(row, tile, s, x)
            return x, q, a, b

        row = pl.ds(0, 8)
        sea_keep(row, 0, 0, surface)
        state = (w / p, sq[row, :], sa[row, :], sb[row, :])
        for s in range(1, 8):
            row = pl.ds(s * 8, 8)
            state = sea_level(row, *state)
            sea_keep(row, 0, s, state[0])
        lax.fori_loop(1, OLEV // 8, sea_down, state)

    sea_copy = pltpu.make_async_copy(sea_w, sea_o, out_sem.at[1])
    sea_copy.start()
    for copy in waiting:
        copy.wait_send()
    air_copy.wait()
    ice_copy.wait()
    sea_copy.wait()


def air_down_again(ag, ab, aw, ay, tile, carry):
    x = list(carry)
    for s in range(8):
        row = pl.ds(pl.multiple_of(tile * 64 + s * 8, 8), 8)
        g, b = ag[row, :], ab[row, :]
        for f in range(4):
            x[f] = g * x[f] + b * aw[f, row, :]
            ay[f, row, :] = x[f]
    return tuple(x)


def lines(value):
    levels, columns = value.shape[-2:]
    tall = min(8, levels)
    return value.reshape(-1, tall, columns // 128, 128).swapaxes(1, 2).reshape(-1, 128)


def unlines(rows, shape):
    levels, columns = shape[-2:]
    return rows.reshape(-1, columns // 128, 8, 128).swapaxes(1, 2).reshape(shape)


def per_device(sections, *args):
    air_state, air_mix, forcing, air_mask, osrc, owt, sea_state, sea_mix, ice, sea_mask, asrc, awt = args
    operands = [
        lines(air_state), lines(air_mix), lines(forcing), air_mask.reshape(8, 128), lines(osrc), lines(owt),
        lines(sea_state), lines(sea_mix), ice.reshape(4, 128), sea_mask.reshape(4, 128), lines(asrc), lines(awt),
    ]
    vmem = [pltpu.VMEM(v.shape, v.dtype) for v in operands[:10]]
    vmem += [pltpu.VMEM((COLS, *v.shape), v.dtype) for v in operands[10:]]
    dma = pltpu.SemaphoreType.DMA
    tall = pltpu.VMEM((8 * OLEV, 128), F32)
    air_one = pltpu.VMEM((8 * LEV, 128), F32)
    air_plus = pltpu.VMEM((8 * LEV + 8, 128), F32)
    air_four = pltpu.VMEM((4, 8 * LEV, 128), F32)
    outs = pl.pallas_call(
        functools.partial(kernel, sections),
        out_shape=[
            jax.ShapeDtypeStruct((2048, 128), F32),
            jax.ShapeDtypeStruct((640, 128), F32),
            jax.ShapeDtypeStruct((4, 128), F32),
        ],
        in_specs=[pl.BlockSpec(memory_space=pltpu.HBM)] * 12,
        out_specs=[pl.BlockSpec(memory_space=pl.ANY)] * 3,
        scratch_shapes=[
            *vmem,
            pltpu.VMEM((STEPS, 8, 128), F32),
            pltpu.VMEM((STEPS, 3 * COLS, 8, 128), F32),
            pltpu.VMEM((STEPS, 3, 5, 8, 128), F32),
            pltpu.VMEM((COLS, 10, 8, 128), F32),
            pltpu.VMEM((STEPS, COLS, 20, 128), F32),
            pltpu.VMEM((STEPS, COLS, 20, 128), F32),
            tall, tall, tall, tall, tall, tall, tall,
            air_one, air_one, air_plus, air_plus, air_one, air_four, air_four,
            pltpu.VMEM((2048, 128), F32), pltpu.VMEM((640, 128), F32), pltpu.VMEM((4, 128), F32),
            dma((12,)), dma((COLS,)), dma((COLS,)), dma((COLS,)), dma((COLS,)),
            dma((STEPS, 11)), dma((STEPS, 12)), dma((STEPS, 2)), dma((STEPS, 3)),
            dma((STEPS, COLS)), dma((STEPS, COLS)), dma((3,)),
        ],
        compiler_params=pltpu.CompilerParams(collective_id=0, has_side_effects=True, vmem_limit_bytes=60 * 2**20),
        cost_estimate=pl.CostEstimate(flops=20_000_000, bytes_accessed=4_000_000, transcendentals=100_000),
        name="coupled",
    )(*operands)
    return unlines(outs[0], air_state.shape), unlines(outs[1], sea_state.shape), outs[2].reshape(512)


def solution(mesh):
    whole = ("sec", "col")
    deep, flat, line = P(None, None, whole), P(None, whole), P(whole)
    return jax.shard_map(
        functools.partial(per_device, mesh.shape["sec"]),
        mesh=mesh,
        in_specs=(deep, flat, flat, line, flat, flat, deep, flat, line, line, flat, flat),
        out_specs=(deep, deep, line),
        check_vma=False,
    )
```

time: 300 us -> 61 us (0.20); the launches traced: 295 us -> 60 us
  other arithmetic: 91.4 us -> 0 us
  local copies, waits for them, and re-layouts: 86.3 us -> 3.66 us
  blocking collectives: 61.3 us -> 0 us
  Pallas kernels: 0 us -> 55.7 us
  starting transfers between devices: 47.7 us -> 0 us
  between operations: 5.51 us -> 0.65 us
  waiting for transfers between devices: 3.17 us -> 0 us
    all_gather x4 -> x0, blocking collectives: 61.3 us -> none  [the longest x2 34.9 us: per_device(): sea_block = lax.all_gather(sea_top, 'col', axis=1, tiled=True)]
    pallas_call x0 -> x1, Pallas kernels: none -> 55.7 us  [per_device(): pl.pallas_call(functools.partial(kernel, sections), out_shape=[jax.ShapeD...]
    ppermute x8 -> x0, starting transfers between devices: 47.7 us -> none  [the longest x4 38.7 us: extended(): after = lax.ppermute(leading, axis, down)]
    gather x4 -> x0, local copies, waits for them, and re-layouts: 47.4 us -> none  [remap(): return jnp.sum(weights[None] * values[:, places], axis=1)]
    unnamed x114 -> x0, other arithmetic: 28.9 us -> none
    add x22 -> x0, other arithmetic: 26.1 us -> none  [solve_columns(): pivot_value = 1.0 + lower_k + upper_k + lower_k * carry_c]
    slice x20 -> x0, local copies, waits for them, and re-layouts: 21.6 us -> none  [the longest x4 12.2 us: solve_columns(): carry_d = (right_side[:, depth_index] + lower_k * carry_d) / pivot_value]
    div x83 -> x0, other arithmetic: 16.5 us -> none  [the longest x8 10.5 us: solve_columns(): carry_d = (right_side[:, depth_index] + lower_k * carry_d) / pivot_value]
  transfers between devices with their start and end apart: 8 -> 0, of which waited for: 1 -> 0; matrix products, arithmetic and copies ran while one was open for 32% -> 0% of each run, Pallas kernels for 0% -> 0%
where the time goes in v1:
time: 61 us; the launch traced here: 60 us
  Pallas kernels  55.7 us (91%)
  local copies, waits for them, and re-layouts  3.66 us (6%)
  between operations  0.65 us (1%)
    pallas_call x1, Pallas kernels, per_device(): pl.pallas_call(functools.partial(kernel, sections), out_shape=[jax.ShapeD...  55.7 us
    unnamed x7, local copies, waits for them, and re-layouts  3.66 us

profile of v1, /device:TPU:1, one launch (start us, length us, event | category | flops | bytes accessed | tf_op | source)
XLA Modules:
  0.0 60.0 jit_solution(17164395030779876571)
XLA Ops:
  0.6 55.7 %coupled.1 = (f32[2048,128]{1,0:T(8,128)}, f32[640,128]{1,0:T(8,128)}, f32[4,128]{1,0:T(4,128)}) custom-call(f32[2048,128]{1,0:T(8,128)} %bitcast.59, f32[512,128]{1,0:T(8,128)} %bitcast.63, f32[32,128]{1,0:T(8,128)} %bitcast.65, s32[8,128]{1,0:T(8,128)} %bitcast.70, s32[32,128]{1,0:T(8,128)} %bitcast.66, f32[32,128]{1,0:T(8,128)} %bitcast.67, ...), custom_call_target="tpu_custom_call" | custom-call | flops 20000000 | bytes 4000000 | tf_op jit(solution)/shard_map/coupled/pallas_call | solution.py:443
  56.4 0.0 copy-start
  56.4 2.4 %copy.23 = f32[4,64,1024]{2,1,0:T(8,128)} copy(f32[4,64,1024]{2,1,0:T(8,128)} %bitcast.60) | data formatting | bytes 2097152
  58.7 0.0 copy-done
  58.7 0.0 copy-start.1
  58.7 0.7 %copy.24 = f32[2,80,512]{2,1,0:T(8,128)} copy(f32[2,80,512]{2,1,0:T(8,128)S(1)} %bitcast.62) | data formatting | bytes 655360
  59.4 0.0 copy-done.1
  59.4 0.6 copy.25
Async XLA Ops:
  56.4 2.4 %copy-start = (f32[640,128]{1,0:T(8,128)S(1)}, f32[640,128]{1,0:T(8,128)}, u32[]{:S(2)}) copy-start(f32[640,128]{1,0:T(8,128)} %get-tuple-element.7) | copy-start | bytes 983044
  58.7 0.7 %copy-start.1 = (f32[4,128]{1,0:T(4,128)S(1)}, f32[4,128]{1,0:T(4,128)}, u32[]{:S(2)}) copy-start(f32[4,128]{1,0:T(4,128)} %get-tuple-element.8) | copy-start | bytes 6148

commit v2 on v1

--- a/solution.py
+++ b/solution.py
@@ -41,11 +41,10 @@
     air_h, amix_h, forcing_h, amask_h, osrc_h, owt_h, sea_h, smix_h, ice_h, smask_h, asrc_h, awt_h,
     air_o, sea_o, ice_o,
     air_v, amix_v, forcing_v, amask_v, osrc_v, owt_v, sea_v, smix_v, ice_v, smask_v, asrc_v, awt_v,
-    top_out, top_in, flux_in, part_acc, part_out, part_in,
+    top_out, top_in, flux_v, part_out, part_in, source_in, weight_in,
     smix8, sdecay8, sea8, sq, sw, sa, sb,
     aq, aa, ag, ab, ae, ay, aw, air_w, sea_w, ice_w,
-    load_sem, src_send, src_recv, wt_send, wt_recv,
-    top_send, top_recv, flux_send, flux_recv, part_send, part_recv, out_sem,
+    load_sem, top_send, top_recv, part_send, part_recv, src_send, src_recv, wt_send, wt_recv, out_sem,
 ):
     sec = lax.axis_index("sec")
     col = lax.axis_index("col")
@@ -53,7 +52,7 @@
     def peer(shift, turn):
         return (lax.rem(sec + shift + sections, sections), lax.rem(col + turn, COLS))
 
-    others = [(s, t) for t in (2, 1, 3, 0) for s in (0, -1, 1) if (s, t) != (0, 0)]
+    others = [(-1, 2), (1, 2), (-1, 1), (1, 1), (-1, 3), (1, 3), (0, 2), (-1, 0), (1, 0), (0, 1), (0, 3)]
 
     barrier = pltpu.get_barrier_semaphore()
     for place in others:
@@ -66,47 +65,62 @@
                 (sea_h, sea_v), (ice_h, ice_v), (osrc_h, osrc_v), (owt_h, owt_v),
                 (forcing_h, forcing_v), (amask_h, amask_v), (amix_h, amix_v), (air_h, air_v),
                 (smix_h, smix_v), (smask_h, smask_v),
-                (asrc_h, asrc_v.at[col]), (awt_h, awt_v.at[col]),
+                (asrc_h, asrc_v), (awt_h, awt_v),
             ]
         )
     ]
     for load in loads:
         load.start()
 
+    one = jnp.ones((8, 128), F32)
+    zero = jnp.zeros((8, 128), F32)
     first = lax.broadcasted_iota(jnp.int32, (8, 128), 0) < 4
     waiting = []
 
-    def send_top(step):
+    def send(block, places, send_sem, recv_sem, make=None):
         for n, (shift, turn) in enumerate(others):
+            slot = (1 - shift) * COLS + col
             copy = pltpu.make_async_remote_copy(
-                src_ref=top_out.at[step],
-                dst_ref=top_in.at[step, (1 - shift) * COLS + col],
-                send_sem=top_send.at[step, n],
-                recv_sem=top_recv.at[step, (1 - shift) * COLS + col],
+                src_ref=make(n, shift, turn) if make else block,
+                dst_ref=places.at[slot],
+                send_sem=send_sem.at[n],
+                recv_sem=recv_sem.at[slot],
                 device_id=peer(shift, turn),
                 device_id_type=MESH,
             )
             copy.start()
             waiting.append(copy)
 
+    def landed(shift, turn, places, recv_sem):
+        slot = (1 + shift) * COLS + lax.rem(col + turn, COLS)
+        block = places.at[slot]
+        pltpu.make_async_copy(block, block, recv_sem.at[slot]).wait()
+        return slot
+
+    def arrivals(step, places, recv_sem, read, count):
+        def one_turn(turn, sums):
+            for shift in (0, -1, 1):
+                slot = (1 + shift) * COLS + lax.rem(col + turn, COLS)
+                if shift or not isinstance(turn, int):
+                    landed(shift, turn, places.at[step], recv_sem.at[step])
+                sums = read(slot, sums)
+            return sums
+
+        sums = one_turn(0, (zero,) * count)
+        return lax.fori_loop(1, COLS, lambda n, sums: one_turn(n + n // 2 - 2 * (n // 3), sums), sums)
+
     loads[0].wait()
     loads[1].wait()
     top_out[0] = jnp.concatenate([sea_v[pl.ds(0, 4, stride=8), :], ice_v[...]], axis=0)
     pl.semaphore_wait(barrier, len(others))
-    send_top(0)
-    for turn in (2, 1, 3):
-        for src, dst, send, recv in ((asrc_h, asrc_v, src_send, src_recv), (awt_h, awt_v, wt_send, wt_recv)):
-            copy = pltpu.make_async_remote_copy(
-                src_ref=src,
-                dst_ref=dst.at[col],
-                send_sem=send.at[turn],
-                recv_sem=recv.at[col],
-                device_id=peer(0, turn),
-                device_id_type=MESH,
-            )
-            copy.start()
-            waiting.append(copy)
-
+    send(top_out.at[0], top_in.at[0], top_send.at[0], top_recv.at[0])
+    loads[10].wait()
+    loads[11].wait()
+    for rows, places in ((asrc_v, source_in), (awt_v, weight_in)):
+        four = [rows[pl.ds(k, 4, stride=4), :] for k in range(4)]
+        places[COLS + col] = jnp.concatenate(four, axis=0)
+    send(source_in.at[COLS + col], source_in, src_send, src_recv)
+    send(weight_in.at[COLS + col], weight_in, wt_send, wt_recv)
     for load in loads[2:10]:
         load.wait()
 
@@ -130,8 +144,6 @@
             ab[below, :] = b * r
         return p, q
 
-    one = jnp.ones((8, 128), F32)
-    zero = jnp.zeros((8, 128), F32)
     pa, qa = lax.fori_loop(0, LEV // 8, air_up, (one, zero))
     inv_pa = 1.0 / pa
 
@@ -187,6 +199,7 @@
     lax.fori_loop(0, OLEV // 8, sea_prepare, 0)
     wet = twice(smask_v[...]) == 1
     ice = twice(ice_v[...])
+
     over_sea = amask_v[...] == 1
     forcing = [forcing_v[pl.ds(f, 8, stride=4), :] for f in range(4)]
     bottom = [air_v[pl.ds(f * 512, 8, stride=8), :] for f in range(4)]
@@ -198,17 +211,18 @@
         source = [osrc_v[pl.ds(k, 8, stride=4), :] for k in range(4)]
         lane = [v & 127 for v in source]
         line = [v >> 7 for v in source]
-        temps, ices = [zero] * 4, [zero] * 4
-        for shift, turn in [(0, 0), *[(s, t) for t in (0, 1, 3, 2) for s in (0, -1, 1) if (s, t) != (0, 0)]]:
-            slot = (1 + shift) * COLS + lax.rem(col + turn, COLS)
-            if (shift, turn) != (0, 0):
-                pltpu.make_async_copy(top_in.at[step, slot], top_in.at[step, slot], top_recv.at[step, slot]).wait()
+        def read_top(slot, sums):
+            sums = list(sums)
             for c in range(4):
                 t, i = top_in[step, slot, pl.ds(c, 1), :], top_in[step, slot, pl.ds(4 + c, 1), :]
                 for k in range(4):
                     here = line[k] == slot * 4 + c
-                    temps[k] = jnp.where(here, lanes(t, lane[k]), temps[k])
-                    ices[k] = jnp.where(here, lanes(i, lane[k]), ices[k])
+                    sums[k] = jnp.where(here, lanes(t, lane[k]), sums[k])
+                    sums[4 + k] = jnp.where(here, lanes(i, lane[k]), sums[4 + k])
+            return tuple(sums)
+
+        picked = arrivals(step, top_in, top_recv, read_top, 8)
+        temps, ices = picked[:4], picked[4:]
         weight = [owt_v[pl.ds(k, 8, stride=4), :] for k in range(4)]
         warm = (weight[0] * temps[0] + weight[1] * temps[1]) + (weight[2] * temps[2] + weight[3] * temps[3])
         cold = (weight[0] * ices[0] + weight[1] * ices[1]) + (weight[2] * ices[2] + weight[3] * ices[3])
@@ -227,48 +241,38 @@
         salt = 0.4 * f1 - forcing[2] * (1.0 - snow)
         melt = 0.5 * heat - 0.8 * (forcing[2] * snow)
         for f, v in enumerate((f2, f3, heat, salt, melt)):
-            flux_in[step, 1, f] = v
-        for n, shift in enumerate((-1, 1)):
-            copy = pltpu.make_async_remote_copy(
-                src_ref=flux_in.at[step, 1],
-                dst_ref=flux_in.at[step, 1 - shift],
-                send_sem=flux_send.at[step, n],
-                recv_sem=flux_recv.at[step, 1 - shift],
-                device_id=peer(shift, 0),
-                device_id_type=MESH,
-            )
-            copy.start()
-            waiting.append(copy)
+            flux_v[f] = v
+
+        def part(shift, turn):
+            slot = (1 + shift) * COLS + lax.rem(col + turn, COLS)
+            index = [source_in[slot, pl.ds(8 * h, 8), :] for h in range(2)]
+            weight = [weight_in[slot, pl.ds(8 * h, 8), :] for h in range(2)]
+            lane = [v & 127 for v in index]
+            line = [(v >> 7) - ((1 - shift) * 32 + 8 * col) for v in index]
+            sums = [zero] * 10
+            for j in range(8):
+                here = [line[h] == j for h in range(2)]
+                for f in range(5):
+                    row = flux_v[f, pl.ds(j, 1), :]
+                    for h in range(2):
+                        sums[2 * f + h] = jnp.where(here[h], lanes(row, lane[h]), sums[2 * f + h])
+            sums = [weight[0] * sums[2 * f] + weight[1] * sums[2 * f + 1] for f in range(5)]
+            sums = [v + pltpu.roll(v, 4, 0) for v in sums]
+            part_out[step, slot, pl.ds(0, 8), :] = jnp.where(first, sums[0], sums[1])
+            part_out[step, slot, pl.ds(8, 8), :] = jnp.where(first, sums[2], sums[3])
+            part_out[step, slot, pl.ds(16, 4), :] = sums[4][0:4]
+            return part_out.at[step, slot]
+
+        def made(n, shift, turn):
+            if step == 0:
+                landed(shift, turn, source_in, src_recv)
+                landed(shift, turn, weight_in, wt_recv)
+            return part(shift, turn)
+
+        send(None, part_in.at[step], part_send.at[step], part_recv.at[step], made)
+        part(0, 0)
         push = (f0, f1, -f2, -f3)
 
-        if step == 0:
-            loads[10].wait()
-            loads[11].wait()
-            for turn in (1, 2, 3):
-                slot = lax.rem(col + turn, COLS)
-                pltpu.make_async_copy(asrc_v.at[slot], asrc_v.at[slot], src_recv.at[slot]).wait()
-                pltpu.make_async_copy(awt_v.at[slot], awt_v.at[slot], wt_recv.at[slot]).wait()
-
-        def picked(target, bands, sums):
-            index = [asrc_v[target, pl.ds(8 * h, 8), :] for h in range(2)]
-            lane = [v & 127 for v in index]
-            line = [(v >> 7) - 8 * col for v in index]
-            for band in bands:
-                for j in range(8):
-                    here = [line[h] == band * 32 + j for h in range(2)]
-                    for f in range(5):
-                        row = flux_in[step, band, f, pl.ds(j, 1), :]
-                        for h in range(2):
-                            sums[f * 2 + h] = jnp.where(here[h], lanes(row, lane[h]), sums[f * 2 + h])
-            return sums
-
-        def own_part(turn, carry):
-            target = lax.rem(col + turn, COLS)
-            for n, v in enumerate(picked(target, (1,), [zero] * 10)):
-                part_acc[turn, n] = v
-            return carry
-
-        lax.fori_loop(0, COLS, own_part, 0)
         if last:
             def air_result(tile, carry):
                 for s in range(8):
@@ -282,37 +286,6 @@
             air_copy = pltpu.make_async_copy(air_w, air_o, out_sem.at[0])
             air_copy.start()
 
-        for band in (0, 2):
-            pltpu.make_async_copy(flux_in.at[step, band], flux_in.at[step, band], flux_recv.at[step, band]).wait()
-
-        def whole_part(target, turn):
-            sums = picked(target, (0, 2), [part_acc[turn, n] for n in range(10)])
-            for f in range(5):
-                done = []
-                for h in range(2):
-                    v = sums[f * 2 + h] * awt_v[target, pl.ds(8 * h, 8), :]
-                    v = v + pltpu.roll(v, 6, 0)
-                    v = v + pltpu.roll(v, 7, 0)
-                    done.append(v)
-                part_out[step, turn, pl.ds(4 * f, 4), :] = jnp.concatenate(
-                    [done[0][0:1], done[0][4:5], done[1][0:1], done[1][4:5]], axis=0
-                )
-
-        for turn in (2, 1, 3, 0):
-            target = lax.rem(col + turn, COLS)
-            whole_part(target, turn)
-            if turn:
-                copy = pltpu.make_async_remote_copy(
-                    src_ref=part_out.at[step, turn],
-                    dst_ref=part_in.at[step, COLS - turn],
-                    send_sem=part_send.at[step, turn],
-                    recv_sem=part_recv.at[step, COLS - turn],
-                    device_id=peer(0, turn),
-                    device_id_type=MESH,
-                )
-                copy.start()
-                waiting.append(copy)
-
         if not last:
             bottom = [ay[f, pl.ds(0, 8), :] + ae[pl.ds(0, 8), :] * push[f] for f in range(4)]
             first_push = push
@@ -323,15 +296,18 @@
 
             top = air_solve(after_first)
 
-        total = part_out[step, 0]
-        for turn in (1, 3, 2):
-            pltpu.make_async_copy(part_in.at[step, turn], part_in.at[step, turn], part_recv.at[step, turn]).wait()
-            total = total + part_in[step, turn]
-        f2, f3, heat, salt, melt = [total[4 * f : 4 * f + 4] for f in range(5)]
-
-        stress = twice(2.0 * jnp.sqrt(f2 * f2 + f3 * f3 + 0.01))
+        if last:
+            for copy in waiting[:-len(others)]:
+                copy.wait_send()
+        total = [part_out[step, COLS + col, pl.ds(8 * n, 8 - n // 2 * 4), :] for n in range(3)]
+        for shift, turn in others[::-1]:
+            slot = landed(shift, turn, part_in.at[step], part_recv.at[step])
+            total = [v + part_in[step, slot, pl.ds(8 * n, 8 - n // 2 * 4), :] for n, v in enumerate(total)]
+
+        winds = total[0] * total[0]
+        stress = 2.0 * jnp.sqrt(winds + pltpu.roll(winds, 4, 0) + 0.01)
         open_water = 1.0 - ice
-        added = open_water * jnp.concatenate([0.5 * heat, 0.3 * salt], axis=0)
+        added = open_water * (jnp.where(first, 0.5, 0.3) * total[1])
         sea8[pl.ds(0, 8), :] = sea8[pl.ds(0, 8), :] + jnp.where(wet, added, 0.0)
 
         def sea_up(n, carry):
@@ -354,11 +330,11 @@
 
         p, q, w = lax.fori_loop(0, OLEV // 8, sea_up, (one, zero, zero))
         surface = jnp.where(wet, w / p, sea8[pl.ds(0, 8), :])
-        grown = ice / (ice + open_water * jnp.exp(twice(melt)))
+        grown = ice / (ice + open_water * jnp.exp(twice(total[2])))
         ice = jnp.where(wet, grown, ice)
         if not last:
             top_out[step + 1] = jnp.where(first, surface, ice)
-            send_top(step + 1)
+            send(top_out.at[step + 1], top_in.at[step + 1], top_send.at[step + 1], top_recv.at[step + 1])
             lax.fori_loop(0, LEV // 8, functools.partial(air_down_again, ag, ab, aw, ay), tuple(top))
         else:
             ice_w[...] = ice[0:4]
@@ -394,15 +370,27 @@
             row = pl.ds(s * 8, 8)
             state = sea_level(row, *state)
             sea_keep(row, 0, s, state[0])
-        lax.fori_loop(1, OLEV // 8, sea_down, state)
-
-    sea_copy = pltpu.make_async_copy(sea_w, sea_o, out_sem.at[1])
-    sea_copy.start()
-    for copy in waiting:
+        middle = OLEV // 16
+        state = lax.fori_loop(1, middle, sea_down, state)
+        if last:
+            sea_copies = []
+            for n in range(2):
+                rows = pl.ds(320 * n, 32 * middle)
+                sea_copies.append(pltpu.make_async_copy(sea_w.at[rows], sea_o.at[rows], out_sem.at[3 + n]))
+                sea_copies[n].start()
+        lax.fori_loop(middle, OLEV // 8, sea_down, state)
+        if last:
+            for n in range(2):
+                rows = pl.ds(320 * n + 32 * middle, 320 - 32 * middle)
+                sea_copies.append(pltpu.make_async_copy(sea_w.at[rows], sea_o.at[rows], out_sem.at[5 + n]))
+                sea_copies[2 + n].start()
+
+    for copy in waiting[-len(others):]:
         copy.wait_send()
     air_copy.wait()
     ice_copy.wait()
-    sea_copy.wait()
+    for copy in sea_copies:
+        copy.wait()
 
 
 def air_down_again(ag, ab, aw, ay, tile, carry):
@@ -416,6 +404,22 @@
     return tuple(x)
 
 
+def hand_on(air, sea, ice, air_o, sea_o, ice_o, air_v, sea_v, ice_v, sem, out_sem):
+    pieces = [(sea, sea_v, sea_o), (ice, ice_v, ice_o)]
+    for n in range(4):
+        rows = pl.ds(512 * n, 512)
+        pieces.append((air.at[rows], air_v.at[rows], air_o.at[rows]))
+    into = [pltpu.make_async_copy(src, mid, sem.at[n]) for n, (src, mid, dst) in enumerate(pieces)]
+    out = [pltpu.make_async_copy(mid, dst, out_sem.at[n]) for n, (src, mid, dst) in enumerate(pieces)]
+    for copy in into:
+        copy.start()
+    for arrive, leave in zip(into, out):
+        arrive.wait()
+        leave.start()
+    for copy in out:
+        copy.wait()
+
+
 def lines(value):
     levels, columns = value.shape[-2:]
     tall = min(8, levels)
@@ -433,8 +437,7 @@
         lines(air_state), lines(air_mix), lines(forcing), air_mask.reshape(8, 128), lines(osrc), lines(owt),
         lines(sea_state), lines(sea_mix), ice.reshape(4, 128), sea_mask.reshape(4, 128), lines(asrc), lines(awt),
     ]
-    vmem = [pltpu.VMEM(v.shape, v.dtype) for v in operands[:10]]
-    vmem += [pltpu.VMEM((COLS, *v.shape), v.dtype) for v in operands[10:]]
+    vmem = [pltpu.VMEM(v.shape, v.dtype) for v in operands]
     dma = pltpu.SemaphoreType.DMA
     tall = pltpu.VMEM((8 * OLEV, 128), F32)
     air_one = pltpu.VMEM((8 * LEV, 128), F32)
@@ -453,21 +456,31 @@
             *vmem,
             pltpu.VMEM((STEPS, 8, 128), F32),
             pltpu.VMEM((STEPS, 3 * COLS, 8, 128), F32),
-            pltpu.VMEM((STEPS, 3, 5, 8, 128), F32),
-            pltpu.VMEM((COLS, 10, 8, 128), F32),
-            pltpu.VMEM((STEPS, COLS, 20, 128), F32),
-            pltpu.VMEM((STEPS, COLS, 20, 128), F32),
+            pltpu.VMEM((5, 8, 128), F32),
+            pltpu.VMEM((STEPS, 3 * COLS, 20, 128), F32),
+            pltpu.VMEM((STEPS, 3 * COLS, 20, 128), F32),
+            pltpu.VMEM((3 * COLS, 16, 128), jnp.int32),
+            pltpu.VMEM((3 * COLS, 16, 128), F32),
             tall, tall, tall, tall, tall, tall, tall,
             air_one, air_one, air_plus, air_plus, air_one, air_four, air_four,
             pltpu.VMEM((2048, 128), F32), pltpu.VMEM((640, 128), F32), pltpu.VMEM((4, 128), F32),
-            dma((12,)), dma((COLS,)), dma((COLS,)), dma((COLS,)), dma((COLS,)),
-            dma((STEPS, 11)), dma((STEPS, 12)), dma((STEPS, 2)), dma((STEPS, 3)),
-            dma((STEPS, COLS)), dma((STEPS, COLS)), dma((3,)),
+            dma((12,)), dma((STEPS, 11)), dma((STEPS, 12)), dma((STEPS, 11)), dma((STEPS, 12)),
+            dma((11,)), dma((12,)), dma((11,)), dma((12,)), dma((7,)),
         ],
         compiler_params=pltpu.CompilerParams(collective_id=0, has_side_effects=True, vmem_limit_bytes=60 * 2**20),
         cost_estimate=pl.CostEstimate(flops=20_000_000, bytes_accessed=4_000_000, transcendentals=100_000),
         name="coupled",
     )(*operands)
+    outs = pl.pallas_call(
+        hand_on,
+        out_shape=[jax.ShapeDtypeStruct(v.shape, F32) for v in outs],
+        in_specs=[pl.BlockSpec(memory_space=pltpu.HBM)] * 3,
+        out_specs=[pl.BlockSpec(memory_space=pltpu.HBM)] * 3,
+        scratch_shapes=[*[pltpu.VMEM(v.shape, F32) for v in outs], dma((6,)), dma((6,))],
+        compiler_params=pltpu.CompilerParams(vmem_limit_bytes=60 * 2**20),
+        cost_estimate=pl.CostEstimate(flops=0, bytes_accessed=3_000_000, transcendentals=0),
+        name="hand_on",
+    )(*outs)
     return unlines(outs[0], air_state.shape), unlines(outs[1], sea_state.shape), outs[2].reshape(512)
 
 

time: 61 us -> 57.4 us (0.941); the launches traced: 60 us -> 57.3 us
  local copies, waits for them, and re-layouts: 3.66 us -> 0 us
  Pallas kernels: 55.7 us -> 56.6 us
    unnamed x7 -> x0, local copies, waits for them, and re-layouts: 3.66 us -> none
    pallas_call x0 -> x1, Pallas kernels: none -> 2.15 us  [per_device(): pl.pallas_call(hand_on, out_shape=[jax.ShapeDtypeStruct(v.shape, F32) for...]
    pallas_call x1, Pallas kernels: 55.7 us -> 54.5 us  [per_device(): pl.pallas_call(functools.partial(kernel, sections), out_shape=[jax.ShapeD...]
where the time goes in v2:
time: 57.4 us; the launch traced here: 57.3 us
  Pallas kernels  56.6 us (99%)
  between operations  0.64 us (1%)
    pallas_call x1, Pallas kernels, per_device(): pl.pallas_call(functools.partial(kernel, sections), out_shape=[jax.ShapeD...  54.5 us
    pallas_call x1, Pallas kernels, per_device(): pl.pallas_call(hand_on, out_shape=[jax.ShapeDtypeStruct(v.shape, F32) for...  2.15 us

profile of v2, /device:TPU:1, one launch (start us, length us, event | category | flops | bytes accessed | tf_op | source)
XLA Modules:
  0.0 57.3 jit_solution(2636279629079485338)
XLA Ops:
  0.6 54.5 %coupled.1 = (f32[2048,128]{1,0:T(8,128)}, f32[640,128]{1,0:T(8,128)}, f32[4,128]{1,0:T(4,128)}) custom-call(f32[2048,128]{1,0:T(8,128)} %bitcast.59, f32[512,128]{1,0:T(8,128)} %bitcast.61, f32[32,128]{1,0:T(8,128)} %bitcast.63, s32[8,128]{1,0:T(8,128)} %bitcast.68, s32[32,128]{1,0:T(8,128)} %bitcast.64, f32[32,128]{1,0:T(8,128)} %bitcast.65, ...), custom_call_target="tpu_custom_call" | custom-call | flops 20000000 | bytes 4000000 | tf_op jit(solution)/shard_map/coupled/pallas_call | solution.py:446
  55.1 2.1 %hand_on.1 = (f32[2048,128]{1,0:T(8,128)}, f32[640,128]{1,0:T(8,128)}, f32[4,128]{1,0:T(4,128)}) custom-call(f32[2048,128]{1,0:T(8,128)} %get-tuple-element.9.air, f32[640,128]{1,0:T(8,128)} %get-tuple-element.10.sea, f32[4,128]{1,0:T(4,128)} %get-tuple-element.11.ice), custom_call_target="tpu_custom_call" | custom-call | bytes 3000000 | tf_op jit(solution)/shard_map/hand_on/pallas_call | solution.py:474

commit v3 on v2

--- a/solution.py
+++ b/solution.py
@@ -41,10 +41,10 @@
     air_h, amix_h, forcing_h, amask_h, osrc_h, owt_h, sea_h, smix_h, ice_h, smask_h, asrc_h, awt_h,
     air_o, sea_o, ice_o,
     air_v, amix_v, forcing_v, amask_v, osrc_v, owt_v, sea_v, smix_v, ice_v, smask_v, asrc_v, awt_v,
-    top_out, top_in, flux_v, part_out, part_in, source_in, weight_in,
+    top_out, top_in, flux_v, part_out, part_in, cells_in,
     smix8, sdecay8, sea8, sq, sw, sa, sb,
     aq, aa, ag, ab, ae, ay, aw, air_w, sea_w, ice_w,
-    load_sem, top_send, top_recv, part_send, part_recv, src_send, src_recv, wt_send, wt_recv, out_sem,
+    load_sem, top_send, top_recv, part_send, part_recv, src_send, src_recv, out_sem,
 ):
     sec = lax.axis_index("sec")
     col = lax.axis_index("col")
@@ -116,11 +116,11 @@
     send(top_out.at[0], top_in.at[0], top_send.at[0], top_recv.at[0])
     loads[10].wait()
     loads[11].wait()
-    for rows, places in ((asrc_v, source_in), (awt_v, weight_in)):
-        four = [rows[pl.ds(k, 4, stride=4), :] for k in range(4)]
-        places[COLS + col] = jnp.concatenate(four, axis=0)
-    send(source_in.at[COLS + col], source_in, src_send, src_recv)
-    send(weight_in.at[COLS + col], weight_in, wt_send, wt_recv)
+    for n, rows in enumerate((asrc_v, awt_v)):
+        four = [rows[pl.ds(k, 4, stride=4), :].astype(F32) for k in range(4)]
+        cells_in[COLS + col, n] = jnp.concatenate(four, axis=0)
+    send(cells_in.at[COLS + col], cells_in, src_send, src_recv)
+
     for load in loads[2:10]:
         load.wait()
 
@@ -245,8 +245,8 @@
 
         def part(shift, turn):
             slot = (1 + shift) * COLS + lax.rem(col + turn, COLS)
-            index = [source_in[slot, pl.ds(8 * h, 8), :] for h in range(2)]
-            weight = [weight_in[slot, pl.ds(8 * h, 8), :] for h in range(2)]
+            index = [cells_in[slot, 0, pl.ds(8 * h, 8), :].astype(jnp.int32) for h in range(2)]
+            weight = [cells_in[slot, 1, pl.ds(8 * h, 8), :] for h in range(2)]
             lane = [v & 127 for v in index]
             line = [(v >> 7) - ((1 - shift) * 32 + 8 * col) for v in index]
             sums = [zero] * 10
@@ -265,8 +265,7 @@
 
         def made(n, shift, turn):
             if step == 0:
-                landed(shift, turn, source_in, src_recv)
-                landed(shift, turn, weight_in, wt_recv)
+                landed(shift, turn, cells_in, src_recv)
             return part(shift, turn)
 
         send(None, part_in.at[step], part_send.at[step], part_recv.at[step], made)
@@ -406,8 +405,8 @@
 
 def hand_on(air, sea, ice, air_o, sea_o, ice_o, air_v, sea_v, ice_v, sem, out_sem):
     pieces = [(sea, sea_v, sea_o), (ice, ice_v, ice_o)]
-    for n in range(4):
-        rows = pl.ds(512 * n, 512)
+    for n in range(8):
+        rows = pl.ds(256 * n, 256)
         pieces.append((air.at[rows], air_v.at[rows], air_o.at[rows]))
     into = [pltpu.make_async_copy(src, mid, sem.at[n]) for n, (src, mid, dst) in enumerate(pieces)]
     out = [pltpu.make_async_copy(mid, dst, out_sem.at[n]) for n, (src, mid, dst) in enumerate(pieces)]
@@ -459,13 +458,12 @@
             pltpu.VMEM((5, 8, 128), F32),
             pltpu.VMEM((STEPS, 3 * COLS, 20, 128), F32),
             pltpu.VMEM((STEPS, 3 * COLS, 20, 128), F32),
-            pltpu.VMEM((3 * COLS, 16, 128), jnp.int32),
-            pltpu.VMEM((3 * COLS, 16, 128), F32),
+            pltpu.VMEM((3 * COLS, 2, 16, 128), F32),
             tall, tall, tall, tall, tall, tall, tall,
             air_one, air_one, air_plus, air_plus, air_one, air_four, air_four,
             pltpu.VMEM((2048, 128), F32), pltpu.VMEM((640, 128), F32), pltpu.VMEM((4, 128), F32),
             dma((12,)), dma((STEPS, 11)), dma((STEPS, 12)), dma((STEPS, 11)), dma((STEPS, 12)),
-            dma((11,)), dma((12,)), dma((11,)), dma((12,)), dma((7,)),
+            dma((11,)), dma((12,)), dma((7,)),
         ],
         compiler_params=pltpu.CompilerParams(collective_id=0, has_side_effects=True, vmem_limit_bytes=60 * 2**20),
         cost_estimate=pl.CostEstimate(flops=20_000_000, bytes_accessed=4_000_000, transcendentals=100_000),
@@ -476,7 +474,7 @@
         out_shape=[jax.ShapeDtypeStruct(v.shape, F32) for v in outs],
         in_specs=[pl.BlockSpec(memory_space=pltpu.HBM)] * 3,
         out_specs=[pl.BlockSpec(memory_space=pltpu.HBM)] * 3,
-        scratch_shapes=[*[pltpu.VMEM(v.shape, F32) for v in outs], dma((6,)), dma((6,))],
+        scratch_shapes=[*[pltpu.VMEM(v.shape, F32) for v in outs], dma((10,)), dma((10,))],
         compiler_params=pltpu.CompilerParams(vmem_limit_bytes=60 * 2**20),
         cost_estimate=pl.CostEstimate(flops=0, bytes_accessed=3_000_000, transcendentals=0),
         name="hand_on",

time: 57.4 us -> 56.8 us (0.990)
  Pallas kernels: 56.6 us -> 56 us
    pallas_call x1, Pallas kernels: 54.5 us -> 53.7 us  [per_device(): pl.pallas_call(functools.partial(kernel, sections), out_shape=[jax.ShapeD...]
where the time goes in v3:
time: 56.8 us; the launch traced here: 56.6 us
  Pallas kernels  56 us (99%)
  between operations  0.64 us (1%)
    pallas_call x1, Pallas kernels, per_device(): pl.pallas_call(functools.partial(kernel, sections), out_shape=[jax.ShapeD...  53.7 us
    pallas_call x1, Pallas kernels, per_device(): pl.pallas_call(hand_on, out_shape=[jax.ShapeDtypeStruct(v.shape, F32) for...  2.22 us

profile of v3, /device:TPU:1, one launch (start us, length us, event | category | flops | bytes accessed | tf_op | source)
XLA Modules:
  0.0 56.6 jit_solution(910955358662818312)
XLA Ops:
  0.6 53.7 %coupled.1 = (f32[2048,128]{1,0:T(8,128)}, f32[640,128]{1,0:T(8,128)}, f32[4,128]{1,0:T(4,128)}) custom-call(f32[2048,128]{1,0:T(8,128)} %bitcast.59, f32[512,128]{1,0:T(8,128)} %bitcast.61, f32[32,128]{1,0:T(8,128)} %bitcast.63, s32[8,128]{1,0:T(8,128)} %bitcast.68, s32[32,128]{1,0:T(8,128)} %bitcast.64, f32[32,128]{1,0:T(8,128)} %bitcast.65, ...), custom_call_target="tpu_custom_call" | custom-call | flops 20000000 | bytes 4000000 | tf_op jit(solution)/shard_map/coupled/pallas_call | solution.py:445
  54.4 2.2 %hand_on.1 = (f32[2048,128]{1,0:T(8,128)}, f32[640,128]{1,0:T(8,128)}, f32[4,128]{1,0:T(4,128)}) custom-call(f32[2048,128]{1,0:T(8,128)} %get-tuple-element.9.air, f32[640,128]{1,0:T(8,128)} %get-tuple-element.10.sea, f32[4,128]{1,0:T(4,128)} %get-tuple-element.11.ice), custom_call_target="tpu_custom_call" | custom-call | bytes 3000000 | tf_op jit(solution)/shard_map/hand_on/pallas_call | solution.py:472
